TPU v7x, 128 devices: a whole 4x4x4 slice. The times are simulated.
128 devices in a mesh: ctx: 32 (over y, z, core), head: 4 (over x).
Axes of the slice: x: 4, y: 4, z: 4, core: 2. Of those that a mesh axis runs over, the one named last changes fastest.
Arguments:
- ctx_hidden: bfloat16 [32768, 4096], P('ctx', 'head')
- resp_hidden: bfloat16 [256, 4096], P('ctx', 'head')
- ctx_pos: int32 [32768], P('ctx'), may hold values from 0 to 65535, as said below
- resp_pos: int32 [256], P('ctx'), may hold values from 65536 to 66047, as said below
- input_norm_gain: float32 [4096], replicated, may hold values from 0.1 to 1.9
- q_weight: bfloat16 [4096, 4096], P(None, 'head'), may hold values from -127 to 127, as said below
- q_scale: float32 [4096], P('head'), as said below
- k_weight: bfloat16 [4096, 512], P(None, 'head'), may hold values from -127 to 127, as said below
- k_scale: float32 [512], P('head'), as said below
- v_weight: bfloat16 [4096, 512], P(None, 'head'), may hold values from -127 to 127, as said below
- v_scale: float32 [512], P('head'), as said below
Outputs:
- ctx_out: bfloat16 [32768, 4096], P('ctx', 'head')
- resp_out: bfloat16 [256, 4096], P('ctx', 'head')
Inputs may be any that keep to these rules, and one draw needn't show every extreme that they name: `ctx_pos`: strictly increasing along the context, consecutive entries differ by 1 to 3. `resp_pos`: strictly increasing, continuing after the last context position, consecutive entries differ by 1 to 3. `q_weight`: whole numbers. `k_weight`: whole numbers. `v_weight`: whole numbers. `q_scale`: Positive. `k_scale`: Positive. `v_scale`: Positive.
All inputs are finite; a program needn't handle non-finite values.
Results may differ from a plain program's by a relative error of at most 0.017.
Values may be sent and summed in bfloat16 or wider, within the bound.
A program may use at most 192 MiB of HBM per device.

v0:
```python
import math

import jax
import jax.numpy as jnp
from jax import lax
from jax.sharding import PartitionSpec as P

HD = 128


EPS = 1e-05
BASE = 500000.0
NEG = -1e30


def spread(value, axis, source):
    kept = jnp.where(lax.axis_index(axis) == source, value, 0).astype(value.dtype)
    return lax.psum(kept, axis)


def combined_all(part, axis, combine):
    gathered = jax.tree.map(lambda a: lax.all_gather(a, axis), part)

    def take(source):
        return jax.tree.map(lambda a: lax.dynamic_index_in_dim(a, source, 0, False), gathered)

    return lax.fori_loop(
        1, lax.axis_size(axis), lambda source, state: combine(state, take(source)), take(0)
    )


def rotate(vectors, positions):
    half_dim = vectors.shape[-1] // 2
    freqs = jnp.exp(
        jnp.arange(half_dim, dtype=jnp.float32) * (-2.0 * math.log(BASE) / vectors.shape[-1])
    )
    angles = positions.astype(jnp.float32)[:, None] * freqs[None, :]
    cosine = jnp.cos(angles)[:, None, :]
    sine = jnp.sin(angles)[:, None, :]
    front_part = vectors[..., :half_dim]
    second = vectors[..., half_dim:]
    return jnp.concatenate(
        [front_part * cosine - second * sine, front_part * sine + second * cosine], axis=-1
    )


def apply_projection(input_rows, input_norm_gain, weight_matrices, weight_scales):
    full_width = input_norm_gain.shape[0]
    whole = lax.all_gather(input_rows, "head", axis=1, tiled=True)
    values = whole.astype(jnp.float32)
    squares = jnp.sum(values * values, axis=1)
    scaled = (values * input_norm_gain[None, :]).astype(jnp.bfloat16)
    projected_rows = tuple(
        (jnp.dot(scaled, matrix, preferred_element_type=jnp.float32) for matrix in weight_matrices)
    )
    inverse = lax.rsqrt(squares / full_width + EPS)
    return tuple(
        (
            projection_output * column_scale[None, :] * inverse[:, None]
            for projection_output, column_scale in zip(projected_rows, weight_scales)
        )
    )


def combine(left, right):
    highest = jnp.maximum(left[0], right[0])
    left_factor = jnp.exp(left[0] - highest)
    right_factor = jnp.exp(right[0] - highest)
    numer = left[1] * left_factor[..., None] + right[1] * right_factor[..., None]
    denom = left[2] * left_factor + right[2] * right_factor
    return (highest, numer, denom)


def local(
    ctx_hidden,
    resp_hidden,
    ctx_pos,
    resp_pos,
    input_norm_gain,
    q_weight,
    q_scale,
    k_weight,
    k_scale,
    v_weight,
    v_scale,
):
    block_rows = ctx_hidden.shape[0]
    resp_rows = resp_hidden.shape[0]
    stacked = jnp.concatenate([ctx_hidden, resp_hidden], axis=0)
    positions = jnp.concatenate([ctx_pos, resp_pos], axis=0)
    total_rows = stacked.shape[0]
    query_proj, key_proj, value_proj = apply_projection(
        stacked, input_norm_gain, (q_weight, k_weight, v_weight), (q_scale, k_scale, v_scale)
    )
    local_heads = query_proj.shape[1] // HD
    local_groups = key_proj.shape[1] // HD
    per_group = local_heads // local_groups
    queries = rotate(query_proj.reshape(total_rows, local_heads, HD), positions).astype(
        jnp.bfloat16
    )
    queries = queries.reshape(total_rows, local_groups, per_group, HD)
    keys_all = rotate(key_proj.reshape(total_rows, local_groups, HD), positions).astype(
        jnp.bfloat16
    )
    values_all = value_proj.reshape(total_rows, local_groups, HD).astype(jnp.bfloat16)
    ctx_keys = keys_all[:block_rows]
    ctx_values = values_all[:block_rows]
    resp_keys = keys_all[block_rows:]
    resp_values = values_all[block_rows:]
    ratio = 1.0 / math.sqrt(HD)
    anchor_keys, anchor_values = (spread(ctx_keys, "ctx", 0), spread(ctx_values, "ctx", 0))
    key_rows = jnp.concatenate([anchor_keys, ctx_keys], axis=0)
    value_rows = jnp.concatenate([anchor_values, ctx_values], axis=0)
    has_anchor = lax.axis_index("ctx") > 0
    block_size = min(block_rows, 512)
    blocks = block_rows // block_size
    ctx_queries = queries[:block_rows].reshape(blocks, block_size, local_groups, per_group, HD)
    key_index = jnp.arange(2 * block_rows, dtype=jnp.int32)

    def attend(operands):
        query_block, offset = operands
        scores = (
            jnp.einsum("nkgd,skd->kgns", query_block, key_rows, preferred_element_type=jnp.float32)
            * ratio
        )
        query_index = offset + jnp.arange(block_size, dtype=jnp.int32)
        from_anchor = (key_index < block_rows)[None, :] & has_anchor
        from_own = (key_index >= block_rows)[None, :] & (
            (key_index - block_rows)[None, :] <= query_index[:, None]
        )
        visible = from_anchor | from_own
        highest = jnp.max(jnp.where(visible, scores, NEG), axis=-1, keepdims=True)
        weights = jnp.where(visible, jnp.exp(scores - highest), 0.0)
        denom = jnp.sum(weights, axis=-1)
        mixed = jnp.einsum(
            "kgns,skd->nkgd",
            weights.astype(jnp.bfloat16),
            value_rows,
            preferred_element_type=jnp.float32,
        )
        return (mixed / jnp.transpose(denom, (2, 0, 1))[..., None]).astype(jnp.bfloat16)

    ctx_out = lax.map(attend, (ctx_queries, jnp.arange(blocks, dtype=jnp.int32) * block_size))
    ctx_out = ctx_out.reshape(block_rows, local_heads * HD)
    gathered = lax.all_gather(queries[block_rows:], "ctx", axis=0, tiled=True)
    all_resp = gathered.shape[0]
    own_first = lax.axis_index("ctx") * resp_rows
    scores_ctx = (
        jnp.einsum("nkgd,skd->kgns", gathered, ctx_keys, preferred_element_type=jnp.float32) * ratio
    )
    scores_resp = (
        jnp.einsum("nkgd,skd->kgns", gathered, resp_keys, preferred_element_type=jnp.float32)
        * ratio
    )
    query_index = jnp.arange(all_resp, dtype=jnp.int32)
    resp_index = own_first + jnp.arange(resp_rows, dtype=jnp.int32)
    causal = resp_index[None, :] <= query_index[:, None]
    highest = jnp.maximum(
        jnp.max(scores_ctx, axis=-1), jnp.max(jnp.where(causal, scores_resp, NEG), axis=-1)
    )
    weights_ctx = jnp.exp(scores_ctx - highest[..., None])
    weights_resp = jnp.where(causal, jnp.exp(scores_resp - highest[..., None]), 0.0)
    denom = jnp.sum(weights_ctx, axis=-1) + jnp.sum(weights_resp, axis=-1)
    numer = jnp.einsum(
        "kgns,skd->nkgd",
        weights_ctx.astype(jnp.bfloat16),
        ctx_values,
        preferred_element_type=jnp.float32,
    )
    numer = numer + jnp.einsum(
        "kgns,skd->nkgd",
        weights_resp.astype(jnp.bfloat16),
        resp_values,
        preferred_element_type=jnp.float32,
    )
    highest = jnp.transpose(highest, (2, 0, 1))
    denom = jnp.transpose(denom, (2, 0, 1))
    merged = combined_all((highest, numer, denom), "ctx", combine)
    merged_num = lax.dynamic_slice_in_dim(merged[1], own_first, resp_rows, 0)
    merged_den = lax.dynamic_slice_in_dim(merged[2], own_first, resp_rows, 0)
    resp_out = (
        (merged_num / merged_den[..., None])
        .astype(jnp.bfloat16)
        .reshape(resp_rows, local_heads * HD)
    )
    return (ctx_out, resp_out)


def solution(mesh):
    return jax.shard_map(
        local,
        mesh=mesh,
        in_specs=(
            P("ctx", "head"),
            P("ctx", "head"),
            P("ctx"),
            P("ctx"),
            P(),
            P(None, "head"),
            P("head"),
            P(None, "head"),
            P("head"),
            P(None, "head"),
            P("head"),
        ),
        out_specs=(P("ctx", "head"), P("ctx", "head")),
        check_vma=False,
    )
```

profile of v0, /device:TPU:1, one launch (start us, length us, event | category | flops | bytes accessed | tf_op | source)
XLA Modules:
  0.0 544.4 jit_solution(537111408415118843)
XLA Ops:
  7.2 3.3 pad_maximum_fusion
  11.4 1.9 multiply_cosine_fusion
  13.3 84.2 %all-gather.7.cloned.1.call-done = bf16[1032,4096]{1,0:T(8,128)(2,1)} async-done(((bf16[1032,1024]{1,0:T(8,128)(2,1)}), bf16[1032,4096]{1,0:T(8,128)(2,1)}) %all-gather.7.cloned.1.call-update) | async-done | bytes 8454160 | tf_op jit(solution)/shard_map/all_gather | solution.py:49
  97.5 5.3 fusion.32
  103.3 3.0 fusion.65
  106.3 1.8 fusion.82
  108.1 9.0 %fusion.71 = f32[129,8,8,128]{3,1,2,0:T(8,128)S(1)} fusion(bf16[4096,1024]{1,0:T(8,128)(2,1)S(1)} %bitcast.214, bf16[1032,4096]{1,0:T(8,128)(2,1)S(1)} %copy-done.4, f32[4096]{0:T(1024)S(1)} %copy-done.11, f32[1032]{0:T(1024)S(1)} %add_rsqrt_fusion, f32[1024]{0:T(1024)S(1)} %copy-done.12), kind=kOutput, calls=%fused_computation.65 | convolution fusion | flops 8671838208 | bytes 21094432 | tf_op jit(solution)/shard_map/dot_general | solution.py:54
  118.1 1.4 fusion.105
  119.5 1.6 add_convert_fusion
  121.3 25.8 %all-gather = bf16[256,8,128]{2,0,1:T(8,128)(2,1)S(1)} all-gather(bf16[8,8,128]{2,0,1:T(8,128)(2,1)S(1)} %pad_maximum_fusion.4), channel_id=2, replica_groups=mesh['ctx'=32,'head'=4] {'ctx'}, dimensions={0}, use_global_device_ids=true | all-gather | bytes 540672 | tf_op jit(solution)/shard_map/all_gather | solution.py:145
  147.1 4.2 fusion.68
  153.2 4.5 bitcast_reduce_fusion
  157.8 5.1 fusion.49
  162.9 1.3 fusion.75
  164.3 4.8 fusion.34
  169.1 24.2 %all-gather.3 = f32[8192,1,8]{0,2,1:T(8,128)S(1)} all-gather(f32[256,1,8]{0,2,1:T(8,128)S(1)} %add_bitcast_fusion), channel_id=5, replica_groups=mesh['ctx'=32,'head'=4] {'ctx'}, dimensions={0}, use_global_device_ids=true | all-gather | bytes 270336 | tf_op jit(solution)/shard_map/all_gather | solution.py:22
  194.0 22.5 %all-gather.1 = f32[8192,1,8]{0,2,1:T(8,128)S(1)} all-gather(f32[256,1,8]{0,2,1:T(8,128)S(1)} %bitcast.211), channel_id=3, replica_groups=mesh['ctx'=32,'head'=4] {'ctx'}, dimensions={0}, use_global_device_ids=true | all-gather | bytes 270336 | tf_op jit(solution)/shard_map/all_gather | solution.py:22
  217.1 3.4 fusion.74
  220.5 40.1 %all-reduce.3.cloned.1.call-done = (bf16[1024,1,128]{0,2,1:T(8,128)(2,1)}, bf16[1024,1,128]{0,2,1:T(8,128)(2,1)}) async-done(((bf16[1024,1,128]{0,2,1:T(8,128)(2,1)}, bf16[1024,1,128]{0,2,1:T(8,128)(2,1)}), (bf16[1024,1,128]{0,2,1:T(8,128)(2,1)}, bf16[1024,1,128]{0,2,1:T(8,128)(2,1)})) %all-reduce.3.cloned.1.call-update) | async-done | bytes 524304 | tf_op jit(solution)/shard_map/psum | solution.py:18
  263.8 100.5 %while.34 = (s32[]{:T(128)}, bf16[2,512,1,8,128]{4,3,1,0,2:T(8,128)(2,1)}, pred[]{:T(512)}, s32[2]{0:T(128)S(1)}, bf16[2,512,1,8,128]{4,1,0,3,2:T(8,128)(2,1)S(1...) while((s32[]{:T(128)}, ...), condition=%wide.region_6.7_spmd.clone.clone, body=%wide.region_3.6_spmd.clone.clone.sunk | while | flops 4391436800 | bytes 126988448 | solution.py:143
  266.1 15.9 %fusion.124 = (f32[8,512]{1,0:T(8,128)S(1)}, f32[512,8,2048]{2,0,1:T(8,128)}) fusion(pred[512,2048]{1,0:T(8,128)(4,1)S(1)} %and_or_fusion.2, bf16[2048,1,128]{2,0,1:T(8,128)(2,1)} %get-tuple-element.533, bf16[2,512,1,8,128]{4,1,0,3,2:T(8,128)(2,1)S(1)} %get-tuple-element.532, s32[]{:T(128)S(6)} %copy.79), kind=kOutput, calls=%fused_computation.13.clone.1 | convolution fusion | flops 2172645376 | bytes 36192260 | tf_op jit(solution)/shard_map/while/body/eval_jaxpr/nkgd,skd->kgns/dot_general | solution.py:123
  282.0 15.5 %fusion.125 = f32[8,512]{1,0:T(8,128)S(1)} fusion(f32[512,8,2048]{2,0,1:T(8,128)} %get-tuple-element.510, f32[8,512]{1,0:T(8,128)S(1)} %get-tuple-element.511, pred[512,2048]{1,0:T(8,128)(4,1)S(1)} %and_or_fusion.2), kind=kLoop, calls=%fused_computation.16.clone.1 | loop fusion | flops 33550336 | bytes 34635776 | tf_op jit(solution)/shard_map/while/body/eval_jaxpr/reduce_sum | solution.py:134
  297.5 14.7 %fusion.126 = bf16[1,512,1,8,128]{4,1,3,2,0:T(8,128)(2,1)S(1)} fusion(f32[512,8,2048]{2,0,1:T(8,128)} %get-tuple-element.510, f32[8,512]{1,0:T(8,128)S(1)} %get-tuple-element.511, pred[512,2048]{1,0:T(8,128)(4,1)S(1)} %and_or_fusion.2, f32[512,8]{0,1:T(8,128)S(1)} %bitcast.209, bf16[2048,1,128]{2,0,1:T(8,128)(2,1)} %get-tuple-element.534), kind=kOutput, calls=%fused_computation.24.clone.1 | convolution fusion | flops 2182086656 | bytes 36208640 | tf_op jit(solution)/shard_map/while/body/eval_jaxpr/kgns,skd->nkgd/dot_general | solution.py:135
  313.0 1.3 copy-done.6
  316.4 15.0 %fusion.124 = (f32[8,512]{1,0:T(8,128)S(1)}, f32[512,8,2048]{2,0,1:T(8,128)}) fusion(pred[512,2048]{1,0:T(8,128)(4,1)S(1)} %and_or_fusion.2, bf16[2048,1,128]{2,0,1:T(8,128)(2,1)} %get-tuple-element.533, bf16[2,512,1,8,128]{4,1,0,3,2:T(8,128)(2,1)S(1)} %get-tuple-element.532, s32[]{:T(128)S(6)} %copy.79), kind=kOutput, calls=%fused_computation.13.clone.1 | convolution fusion | flops 2172645376 | bytes 36192260 | tf_op jit(solution)/shard_map/while/body/eval_jaxpr/nkgd,skd->kgns/dot_general | solution.py:123
  331.3 16.4 %fusion.125 = f32[8,512]{1,0:T(8,128)S(1)} fusion(f32[512,8,2048]{2,0,1:T(8,128)} %get-tuple-element.510, f32[8,512]{1,0:T(8,128)S(1)} %get-tuple-element.511, pred[512,2048]{1,0:T(8,128)(4,1)S(1)} %and_or_fusion.2), kind=kLoop, calls=%fused_computation.16.clone.1 | loop fusion | flops 33550336 | bytes 34635776 | tf_op jit(solution)/shard_map/while/body/eval_jaxpr/reduce_sum | solution.py:134
  347.8 14.3 %fusion.126 = bf16[1,512,1,8,128]{4,1,3,2,0:T(8,128)(2,1)S(1)} fusion(f32[512,8,2048]{2,0,1:T(8,128)} %get-tuple-element.510, f32[8,512]{1,0:T(8,128)S(1)} %get-tuple-element.511, pred[512,2048]{1,0:T(8,128)(4,1)S(1)} %and_or_fusion.2, f32[512,8]{0,1:T(8,128)S(1)} %bitcast.209, bf16[2048,1,128]{2,0,1:T(8,128)(2,1)} %get-tuple-element.534), kind=kOutput, calls=%fused_computation.24.clone.1 | convolution fusion | flops 2182086656 | bytes 36208640 | tf_op jit(solution)/shard_map/while/body/eval_jaxpr/kgns,skd->nkgd/dot_general | solution.py:135
  362.9 1.3 copy-done.6
  364.3 3.6 copy.66
  367.9 21.0 %all-gather.9.cloned.1.call-done = f32[8192,1,8,128]{0,3,2,1:T(8,128)} async-done(((f32[256,1,8,128]{0,3,2,1:T(8,128)}), f32[8192,1,8,128]{0,3,2,1:T(8,128)}) %all-gather.9.cloned.1.call-update) | async-done | bytes 33554448 | tf_op jit(solution)/shard_map/all_gather | solution.py:22
  388.9 1.3 slice.67
  390.6 33.5 %copy.50 = f32[8192,1,8,128]{3,2,0,1:T(8,128)} copy(f32[8192,1,8,128]{0,3,2,1:T(8,128)} %all-gather.9.cloned.1.call-done) | data formatting | bytes 67108864 | tf_op jit(solution)/shard_map/while | solution.py:27
  424.2 112.6 %while.33 = (s32[]{:T(128)}, f32[256,1,8]{0,2,1:T(8,128)S(1)}, f32[256,1,8,128]{3,2,1,0:T(8,128)S(1)}, f32[256,1,8]{0,2,1:T(8,128)S(1)}, f32[32,256,1,8]{1,3,2,0...) while((s32[]{:T(128)}, f32[256,1,8]{0,2,1:T(8,128)S(1)}, ...), condition=%wide.region_12.13_spmd, body=%wide.region_11.12_spmd.sunk | while | flops 802821 | bytes 3301523 | solution.py:27
  426.0 1.9 fusion.121
  429.6 1.9 fusion.121
  433.2 1.9 fusion.121
  436.9 1.9 fusion.121
  440.5 1.9 fusion.121
  444.1 1.9 fusion.121
  447.7 1.9 fusion.121
  451.4 1.9 fusion.121
  455.0 1.9 fusion.121
  458.6 1.9 fusion.121
  462.3 1.9 fusion.121
  465.9 1.9 fusion.121
  469.5 1.9 fusion.121
  473.2 1.9 fusion.121
  476.8 1.9 fusion.121
  480.4 1.9 fusion.121
  484.0 1.9 fusion.121
  487.7 1.9 fusion.121
  491.3 1.9 fusion.121
  494.9 1.9 fusion.121
  498.6 1.9 fusion.121
  502.2 1.9 fusion.121
  505.8 1.9 fusion.121
  509.5 1.9 fusion.121
  513.1 1.9 fusion.121
  516.7 1.9 fusion.121
  520.3 1.9 fusion.121
  524.0 1.9 fusion.121
  527.6 1.9 fusion.121
  531.2 1.9 fusion.121
  534.9 1.9 fusion.121
  (235 shorter events, 68.5 us)
Async XLA Ops:
  7.2 95.7 %copy-start = (bf16[4096,128]{1,0:T(8,128)(2,1)S(1)}, bf16[4096,128]{1,0:T(8,128)(2,1)}, u32[]{:S(2)}) copy-start(bf16[4096,128]{1,0:T(8,128)(2,1)} %param.22) | copy-start | bytes 3145732
  7.2 95.6 %copy-start.11 = (f32[4096]{0:T(1024)S(1)}, f32[4096]{0:T(1024)}, u32[]{:S(2)}) copy-start(f32[4096]{0:T(1024)} %param.19) | copy-start | bytes 49156
  7.2 95.6 %copy-start.13 = (f32[128]{0:T(128)S(1)}, f32[128]{0:T(128)}, u32[]{:S(2)}) copy-start(f32[128]{0:T(128)} %param.23) | copy-start | bytes 1540
  7.2 90.3 %all-gather.7.cloned.1.call-start = ((), (), s32[]{:S(2)}) async-start(), calls=%async_computation | async-start | bytes 10567680 | tf_op jit(solution)/shard_map/all_gather | solution.py:49
  10.5 250.1 %all-reduce.3.cloned.1.call-start = ((), (), s32[]{:S(2)}) async-start(), calls=%async_computation.2 | async-start | bytes 1048576 | tf_op jit(solution)/shard_map/psum | solution.py:18
  97.5 5.8 %copy-start.4 = (bf16[1032,4096]{1,0:T(8,128)(2,1)S(1)}, bf16[1032,4096]{1,0:T(8,128)(2,1)}, u32[]{:S(2)}) copy-start(bf16[1032,4096]{1,0:T(8,128)(2,1)} %all-gather.7.cloned.1.call-done) | copy-start | bytes 25362436
  97.5 10.5 %slice-start = ((s8[8388608]{0:T(1024)(128)(4,1)}), s8[4194304]{0:T(1024)(128)(4,1)S(1)}, s32[]{:S(2)}) async-start(s8[8388608]{0:T(1024)(128)(4,1)} %bitcast.213), calls=%async_computation.3 | async-start | bytes 8388608
  103.3 4.7 slice-start.1
  103.3 4.7 copy-start.12
  119.5 27.6 %copy-start.14 = (f32[128]{0:T(128)S(1)}, f32[128]{0:T(128)}, u32[]{:S(2)}) copy-start(f32[128]{0:T(128)} %param.25) | copy-start | bytes 1540
  121.2 30.1 %copy-start.2 = (bf16[1032,8,64]{2,0,1:T(8,128)(2,1)}, bf16[1032,8,64]{2,0,1:T(8,128)(2,1)S(1)}, u32[]{:S(2)}) copy-start(bf16[1032,8,64]{2,0,1:T(8,128)(2,1)S(1)} %get-tuple-element.394) | copy-start | bytes 3170308
  121.2 30.1 %copy-start.3 = (bf16[1032,8,64]{2,0,1:T(8,128)(2,1)}, bf16[1032,8,64]{2,0,1:T(8,128)(2,1)S(1)}, u32[]{:S(2)}) copy-start(bf16[1032,8,64]{2,0,1:T(8,128)(2,1)S(1)} %get-tuple-element.395) | copy-start | bytes 3170308
  157.8 231.1 %all-gather.9.cloned.1.call-start = ((), (), s32[]{:S(2)}) async-start(), calls=%async_computation.1 | async-start | bytes 34603008 | tf_op jit(solution)/shard_map/all_gather | solution.py:22
  193.3 0.7 copy-start.10
  216.5 44.1 %copy-start.8 = (f32[8192,1,8]{0,2,1:T(8,128)}, f32[8192,1,8]{0,2,1:T(8,128)S(1)}, u32[]{:S(2)}) copy-start(f32[8192,1,8]{0,2,1:T(8,128)S(1)} %all-gather.1) | copy-start | bytes 786436
  297.5 14.7 %copy-start.5 = (bf16[2,512,1,8,128]{4,3,1,0,2:T(8,128)(2,1)S(1)}, bf16[2,512,1,8,128]{4,3,1,0,2:T(8,128)(2,1)}, u32[]{:S(2)}) copy-start(bf16[2,512,1,8,128]{4,3,1,0,2:T(8,128)(2,1)} %get-tuple-element.521) | copy-start | bytes 6291460 | tf_op jit(solution)/shard_map/while
  313.0 1.3 copy-start.6
  347.8 14.4 %copy-start.5 = (bf16[2,512,1,8,128]{4,3,1,0,2:T(8,128)(2,1)S(1)}, bf16[2,512,1,8,128]{4,3,1,0,2:T(8,128)(2,1)}, u32[]{:S(2)}) copy-start(bf16[2,512,1,8,128]{4,3,1,0,2:T(8,128)(2,1)} %get-tuple-element.521) | copy-start | bytes 6291460 | tf_op jit(solution)/shard_map/while
  362.9 1.3 copy-start.6
  390.6 33.5 %copy-start.7 = (f32[256,1,8]{0,2,1:T(8,128)S(1)}, f32[256,1,8]{0,2,1:T(8,128)}, u32[]{:S(2)}) copy-start(f32[256,1,8]{0,2,1:T(8,128)} %slice.65) | copy-start | bytes 24580
  390.6 33.5 %copy-start.9 = (f32[256,1,8]{0,2,1:T(8,128)S(1)}, f32[256,1,8]{0,2,1:T(8,128)}, u32[]{:S(2)}) copy-start(f32[256,1,8]{0,2,1:T(8,128)} %slice.68) | copy-start | bytes 24580
  424.1 113.5 %copy-start.1 = (bf16[4096,128]{1,0:T(8,128)(2,1)S(1)}, bf16[4096,128]{1,0:T(8,128)(2,1)}, u32[]{:S(2)}) copy-start(bf16[4096,128]{1,0:T(8,128)(2,1)} %param.22) | copy-start | bytes 3145732
Sparse Core Ops, SparseCore 0:
  10.7 86.8 all-gather.6
  157.9 102.6 all-reduce.2
  263.0 125.8 all-gather.8
where the time goes:
time: 555 us; the launch traced here: 544 us
  other arithmetic  164 us (30%)
  waiting for transfers between devices  145 us (26%)
  matrix products  87.2 us (16%)
  blocking collectives  72.5 us (13%)
  local copies, waits for them, and re-layouts  59 us (11%)
  between operations  14.3 us (3%)
    all_gather x1, waiting for transfers between devices, apply_projection(): whole = lax.all_gather(input_rows, 'head', axis=1, tiled=True)  84.2 us
    add x31, other arithmetic, combine(): left[1] * left_factor[..., None] + right[1] * right_factor[..., None]  58.7 us
    all_gather x2, blocking collectives, combined_all(): gathered = jax.tree.map(lambda a: lax.all_gather(a, axis), part)  46.7 us
    psum x1, waiting for transfers between devices, spread(): return lax.psum(kept, axis)  40.1 us
    while x3, local copies, waits for them, and re-layouts, combined_all(): lax.fori_loop(1, lax.axis_size(axis), lambda source, state: combine(state...  34 us
    reduce_sum x2, other arithmetic, attend(): denom = jnp.sum(weights, axis=-1)  31.9 us
    dot_general x2, matrix products, attend(): jnp.einsum('nkgd,skd->kgns', query_block, key_rows, preferred_element_typ...  30.8 us
    dot_general x2, matrix products, attend(): jnp.einsum('kgns,skd->nkgd', weights.astype(jnp.bfloat16), value_rows, pr...  29 us
  transfers between devices with their start and end apart: 3, of which 3 were waited for; matrix products, arithmetic and copies ran while one was open for 23% of the time, Pallas kernels for 0%

commit v1 on v0

v1 whole, which is shorter than its diff:
```python
import functools
import math

import jax
import jax.numpy as jnp
import numpy as np
from jax import lax
from jax.experimental import pallas as pl
from jax.experimental.pallas import tpu as pltpu
from jax.sharding import PartitionSpec as P

HD = 128
EPS = 1e-05
BASE = 500000.0
NEG = -1e30
RD = 8
MESH = pl.DeviceIdType.MESH
F32 = jnp.float32
BF16 = jnp.bfloat16
NX = 4


def nt(a, b):
    return lax.dot_general(a, b, (((1,), (1,)), ((), ())), preferred_element_type=F32)


def nn(a, b):
    return jnp.dot(a, b, preferred_element_type=F32)


def iota(shape, dim):
    return lax.broadcasted_iota(jnp.int32, shape, dim)


def kernel(
    n_ctx,
    chunks,
    hidden,
    resp_hidden,
    pos,
    resp_pos,
    gain,
    qw,
    kw,
    vw,
    q_scale,
    k_scale,
    v_scale,
    freq,
    ctx_out,
    resp_out,
    W,
    G,
    XS,
    SC,
    SCS,
    PF,
    PA,
    TC,
    TS,
    AG,
    KA,
    VA,
    RQ,
    K,
    V,
    KR,
    VR,
    Q,
    OUT,
    RM,
    RN,
    SB,
    RB,
    AUX,
    WT,
    lsem,
    scat_send,
    scat_recv,
    small_send,
    small_recv,
    ag_send,
    ag_recv,
    g_send,
    g_recv,
    r_send,
    r_recv,
    o_sem,
):
    blk, fs = hidden.shape
    full = NX * fs
    qc = q_scale.shape[1]
    heads = qc // HD
    ap = blk // n_ctx
    rr = heads * RD
    n_chunks = len(chunks)
    c = lax.axis_index("ctx")
    h = lax.axis_index("head")
    right = lax.rem(h + 1, NX)
    opp = lax.rem(h + 2, NX)
    left = lax.rem(h + 3, NX)

    loads = [
        pltpu.make_async_copy(qw, W.at[:, pl.ds(0, qc)], lsem.at[0]),
        pltpu.make_async_copy(kw, W.at[:, pl.ds(qc, HD)], lsem.at[1]),
        pltpu.make_async_copy(vw, W.at[:, pl.ds(qc + HD, HD)], lsem.at[2]),
        pltpu.make_async_copy(hidden, G.at[h], lsem.at[3]),
    ]

    barrier = pltpu.get_barrier_semaphore()

    def greet(d, carry):
        pl.semaphore_signal(
            barrier, inc=1, device_id=(lax.rem(c + d, n_ctx), h), device_id_type=MESH
        )
        return carry

    lax.fori_loop(1, n_ctx, greet, 0)
    for x in (left, right, opp):
        pl.semaphore_signal(barrier, inc=1, device_id=(c, x), device_id_type=MESH)
    PF[...] = pos[...].astype(F32)
    pl.semaphore_wait(barrier, n_ctx - 1 + 3)

    def remote(src, dst, ssem, rsem, dev):
        return pltpu.make_async_remote_copy(
            src_ref=src, dst_ref=dst, send_sem=ssem, recv_sem=rsem,
            device_id=dev, device_id_type=MESH,
        )

    def wait_bytes(ref, sem):
        pltpu.make_async_copy(ref, ref, sem).wait()

    def scat(d):
        return (
            remote(hidden.at[pl.ds(pl.multiple_of(d * ap, ap), ap)], XS.at[h, pl.ds(0, ap)],
                   scat_send.at[0], scat_recv.at[0], (d, h)),
            remote(PF, PA, scat_send.at[1], scat_recv.at[1], (d, h)),
        )

    own_piece = pltpu.make_async_copy(
        hidden.at[pl.ds(0, ap)], XS.at[h, pl.ds(0, ap)], lsem.at[4]
    )

    @pl.when(c == 0)
    def _():
        def go(d, carry):
            for copy in scat(d):
                copy.start()
            return carry

        lax.fori_loop(1, n_ctx, go, 0)
        own_piece.start()

    def own(j):
        r0, n = chunks[j]
        rows = pl.ds(r0, n)
        return (
            remote(hidden.at[rows], G.at[h, rows], g_send.at[j, 0], g_recv.at[j, 0], (c, right)),
            remote(hidden.at[rows], G.at[h, rows], g_send.at[j, 1], g_recv.at[j, 1], (c, left)),
        )

    def fwd(j):
        r0, n = chunks[j]
        a, b = pl.ds(r0, n // 2), pl.ds(r0 + n // 2, n // 2)
        return (
            remote(G.at[left, a], G.at[left, a], g_send.at[j, 2], g_recv.at[j, 2], (c, right)),
            remote(G.at[right, b], G.at[right, b], g_send.at[j, 3], g_recv.at[j, 3], (c, left)),
        )

    def start_own(j):
        if j < n_chunks:
            for copy in own(j):
                copy.start()

    def turn(j):
        if j < n_chunks:
            for copy in own(j):
                copy.wait_recv()
            for copy in fwd(j):
                copy.start()

    start_own(0)
    for copy in loads:
        copy.start()

    lane = iota((1, HD), 1)
    sign = jnp.where(lane < HD // 2, -1.0, 1.0).astype(F32)

    def tables(t, carry):
        column = jnp.transpose(jnp.broadcast_to(PF[pl.ds(t, 1), :], (HD, HD)))
        angle = column * freq[...]
        rows = pl.ds(pl.multiple_of(t * HD, HD), HD)
        TC[rows, :] = jnp.cos(angle)
        TS[rows, :] = jnp.sin(angle) * sign
        return carry

    lax.fori_loop(0, blk // HD, tables, 0)
    V[:, pl.ds(HD, HD)] = jnp.ones((blk, HD), BF16)
    VA[:, pl.ds(HD, HD)] = jnp.ones((blk, HD), BF16)
    KR[...] = jnp.zeros(KR.shape, BF16)
    VR[...] = jnp.zeros(VR.shape, BF16)
    WT[...] = jnp.zeros(WT.shape, F32)

    resp_rows = resp_hidden[...].astype(F32)
    XS[h, pl.ds(ap, 16), :] = jnp.concatenate([resp_rows, jnp.zeros_like(resp_rows)], 0).astype(BF16)

    @pl.when(c == 0)
    def _():
        PA[...] = PF[...]
        own_piece.wait()

    @pl.when(c > 0)
    def _():
        for copy in scat(0):
            copy.wait_recv()

    small = [
        remote(XS.at[h], XS.at[h], small_send.at[k], small_recv.at[k], (c, x))
        for k, x in enumerate((right, opp, left))
    ]
    for copy in small:
        copy.start()
    start_own(1)
    turn(0)
    start_own(2)

    def rotated(x, cosine, sine):
        return x * cosine + pltpu.roll(x, HD // 2, 1) * sine

    fold = math.log2(math.e) / math.sqrt(HD)

    anchor_pos = jnp.sum(
        jnp.where(
            iota((ap, HD), 1) == lax.rem(c * ap, HD) + iota((ap, HD), 0),
            jnp.broadcast_to(PA[pl.ds((c * ap) // HD, 1), :], (ap, HD)),
            0.0,
        ),
        axis=1, keepdims=True,
    )
    own_resp_pos = jnp.sum(
        jnp.where(
            iota((16, RD), 1) == iota((16, RD), 0),
            jnp.broadcast_to(resp_pos[...].astype(F32), (16, RD)),
            0.0,
        ),
        axis=1, keepdims=True,
    )
    angle = jnp.concatenate([anchor_pos, own_resp_pos], 0) * freq[...]
    small_cos = jnp.cos(angle)
    small_sin = jnp.sin(angle) * sign
    for copy in small:
        copy.wait_recv()
    for copy in loads:
        copy.wait()

    def scale_rows(src, rows, dst, n):
        squares = jnp.zeros((n, 1), F32)
        for s in range(NX):
            x = src[s, rows, :].astype(F32)
            squares += jnp.sum(x * x, axis=1, keepdims=True)
            dst[pl.ds(0, n), pl.ds(s * fs, fs)] = (x * gain[:, pl.ds(s * fs, fs)]).astype(BF16)
        return lax.rsqrt(squares / full + EPS)

    inverse = scale_rows(XS, pl.ds(0, ap + 16), SCS, ap + 16)
    small_cos = small_cos * inverse
    small_sin = small_sin * inverse
    kv = nn(SCS[...], W[:, pl.ds(qc, 2 * HD)])
    keys = rotated(kv[:, :HD] * k_scale[...], small_cos, small_sin)
    values = kv[:, HD:] * v_scale[...] * inverse
    AG[0, pl.ds(0, ap), :] = keys[:ap].astype(BF16)
    AG[0, pl.ds(ap, ap), :] = values[:ap].astype(BF16)
    KR[pl.ds(0, 16), :] = keys[ap:].astype(BF16)
    VR[pl.ds(0, 16), pl.ds(0, HD)] = values[ap:].astype(BF16)
    VR[pl.ds(0, 16), pl.ds(HD, HD)] = jnp.ones((16, HD), BF16)
    pieces = []
    for t in range(qc // (2 * HD)):
        cols = pl.ds(t * 2 * HD, 2 * HD)
        part = nn(SCS[pl.ds(ap, 16), :], W[:, cols]) * (q_scale[:, cols] * fold)
        for k in range(2):
            pieces.append(
                rotated(part[:, k * HD:(k + 1) * HD], small_cos[ap:], small_sin[ap:])[:RD]
            )
    AG[0, pl.ds(2 * ap, rr), :] = jnp.concatenate(pieces, 0).astype(BF16)

    def spread(d):
        return remote(AG.at[0], AG.at[d], ag_send.at[0], ag_recv.at[0],
                      (lax.rem(c + n_ctx - d, n_ctx), h))

    def send_spread(d, carry):
        spread(d).start()
        return carry

    lax.fori_loop(1, n_ctx, send_spread, 0)

    def project_kv(j, inverse, cosine, sine):
        r0, n = chunks[j]
        kv = nn(SC[pl.ds(0, n), :], W[:, pl.ds(qc, 2 * HD)])
        K[pl.ds(r0, n), :] = rotated(kv[:, :HD] * k_scale[...], cosine, sine).astype(BF16)
        V[pl.ds(r0, n), pl.ds(0, HD)] = (kv[:, HD:] * v_scale[...] * inverse).astype(BF16)

    def project_q(j, cosine, sine):
        r0, n = chunks[j]

        def step(t, carry):
            cols = pl.ds(pl.multiple_of(t * 2 * HD, 2 * HD), 2 * HD)
            part = nn(SC[pl.ds(0, n), :], W[:, cols]) * (q_scale[:, cols] * fold)
            for k in range(2):
                Q[2 * t + k, pl.ds(0, n), :] = rotated(
                    part[:, k * HD:(k + 1) * HD], cosine, sine
                ).astype(BF16)
            return carry

        lax.fori_loop(0, qc // (2 * HD), step, 0)

    def attend(j, with_anchor):
        r0, n = chunks[j]
        hs = max(1, min(heads, 256 // n))
        visible = iota((hs * n, n), 1) <= lax.rem(iota((hs * n, n), 0), n)

        def step(i, carry):
            q = Q[pl.ds(i * hs, hs), pl.ds(0, n), :].reshape(hs * n, HD)
            scores = [jnp.where(visible, nt(q, K[pl.ds(r0, n), :]), NEG)]
            vals = [V[pl.ds(r0, n), :]]
            if r0:
                scores.append(nt(q, K[pl.ds(0, r0), :]))
                vals.append(V[pl.ds(0, r0), :])
            if with_anchor:
                scores.append(nt(q, KA[...]))
                vals.append(VA[...])
            top = functools.reduce(
                jnp.maximum, [jnp.max(s, axis=1, keepdims=True) for s in scores]
            )
            total = None
            for s, v in zip(scores, vals):
                part = nn(jnp.exp2(s - top).astype(BF16), v)
                total = part if total is None else total + part
            mixed = (total[:, :HD] / total[:, HD:]).astype(BF16)
            for k in range(hs):
                OUT[pl.ds(r0, n), pl.ds(pl.multiple_of((i * hs + k) * HD, HD), HD)] = (
                    mixed[k * n:(k + 1) * n]
                )
            return carry

        lax.fori_loop(0, heads // hs, step, 0)

    def out_copy(j):
        r0, n = chunks[j]
        return pltpu.make_async_copy(
            OUT.at[pl.ds(r0, n)], ctx_out.at[pl.ds(r0, n)], o_sem.at[j]
        )

    ts = min(n_ctx, 256 // rr)
    tr = ts * rr
    last0, last_n = chunks[-1]

    def resp_first(i, carry):
        rows = pl.ds(pl.multiple_of(i * tr, tr), tr)
        q = RQ[rows, :]
        row = iota((tr, HD), 0)
        col = iota((tr, HD), 1)
        src = c + i * ts + row // rr
        src = jnp.where(src >= n_ctx, src - n_ctx, src)
        query = lax.rem(row, RD)
        seen = (col < RD) & (c * RD + col <= src * RD + query)
        s_own = jnp.where(seen, nt(q, KR[...]), NEG)
        s_ctx = nt(q, K[pl.ds(0, last0), :])
        top = jnp.maximum(
            jnp.max(s_own, axis=1, keepdims=True), jnp.max(s_ctx, axis=1, keepdims=True)
        )
        RN[rows, :] = nn(jnp.exp2(s_own - top).astype(BF16), VR[...]) + nn(
            jnp.exp2(s_ctx - top).astype(BF16), V[pl.ds(0, last0), :]
        )
        RM[rows, :] = jnp.broadcast_to(top, (tr, HD))
        return carry

    def give(d):
        return remote(SB.at[d], RB.at[n_ctx - 1 - d], r_send.at[0], r_recv.at[0],
                      (lax.rem(c + d, n_ctx), h))

    def resp_second(i, carry):
        rows = pl.ds(pl.multiple_of(i * tr, tr), tr)
        q = RQ[rows, :]
        s = nt(q, K[pl.ds(last0, last_n), :])
        before = RM[rows, :]
        top = jnp.maximum(before, jnp.max(s, axis=1, keepdims=True))
        factor = jnp.exp2(before - top)
        part = nn(jnp.exp2(s - top[:, :1]).astype(BF16), V[pl.ds(last0, last_n), :])
        num = RN[rows, pl.ds(0, HD)] * factor + part[:, :HD]
        den = RN[rows, pl.ds(HD, HD)] * factor + part[:, HD:]
        row = iota((rr, HD), 0)
        col = iota((rr, HD), 1)
        sub = iota((16, HD), 0)
        for k in range(ts):
            d = i * ts + k
            own_rows = slice(k * rr, (k + 1) * rr)
            SB[d, pl.ds(0, rr), :] = num[own_rows].astype(BF16)
            both = jnp.where(col == row, top[own_rows], 0.0) + jnp.where(
                col == row + 64, den[own_rows], 0.0
            )
            both = jnp.sum(both, axis=0, keepdims=True)
            high = both.astype(BF16).astype(F32)
            mid = (both - high).astype(BF16).astype(F32)
            low = both - high - mid
            SB[d, pl.ds(rr, 16), :] = jnp.where(
                sub == 0, high, jnp.where(sub == 1, mid, jnp.where(sub == 2, low, 0.0))
            ).astype(BF16)

            @pl.when(d > 0)
            def _():
                give(d).start()

        return carry

    def gathered():
        wait_bytes(AG.at[pl.ds(1, n_ctx - 1)], ag_recv.at[0])

        def place(d, carry):
            rows = pl.ds(pl.multiple_of(d * ap, ap), ap)
            KA[rows, :] = AG[d, pl.ds(0, ap), :]
            VA[rows, pl.ds(0, HD)] = AG[d, pl.ds(ap, ap), :]
            RQ[pl.ds(pl.multiple_of(d * rr, rr), rr), :] = AG[d, pl.ds(2 * ap, rr), :]
            return carry

        lax.fori_loop(0, n_ctx, place, 0)

    for j in range(n_chunks):
        r0, n = chunks[j]
        turn(j + 1)
        start_own(j + 3)
        for copy in fwd(j):
            copy.wait_recv()
        inverse = scale_rows(G, pl.ds(r0, n), SC, n)
        cosine = TC[pl.ds(r0, n), :] * inverse
        sine = TS[pl.ds(r0, n), :] * inverse
        project_kv(j, inverse, cosine, sine)
        if j == n_chunks - 1:
            lax.fori_loop(0, n_ctx // ts, resp_second, 0)
        project_q(j, cosine, sine)
        if j == 0:
            gathered()

        @pl.when(c > 0)
        def _():
            attend(j, True)

        @pl.when(c == 0)
        def _():
            attend(j, False)

        out_copy(j).start()
        if j == n_chunks - 2:
            lax.fori_loop(0, n_ctx // ts, resp_first, 0)

    wait_bytes(RB, r_recv.at[0])

    def unpack(k, carry):
        AUX[pl.ds(k, 1), :] = jnp.sum(RB[k, pl.ds(rr, 16), :].astype(F32), axis=0, keepdims=True)
        return carry

    lax.fori_loop(0, n_ctx - 1, unpack, 0)
    AUX[pl.ds(n_ctx - 1, 1), :] = jnp.sum(
        SB[0, pl.ds(rr, 16), :].astype(F32), axis=0, keepdims=True
    )
    both = AUX[...]
    weight = jnp.exp2(both - jnp.max(both, axis=0, keepdims=True))
    den = jnp.sum(weight * pltpu.roll(both, HD // 2, 1), axis=0, keepdims=True)
    WT[pl.ds(0, n_ctx), :] = jnp.where(iota((n_ctx, HD), 1) < rr, weight / den, 0.0)
    turned = jnp.transpose(WT[...])
    total = turned[:rr, n_ctx - 1:n_ctx] * SB[0, pl.ds(0, rr), :].astype(F32)
    for k in range(n_ctx - 1):
        total += turned[:rr, k:k + 1] * RB[k, pl.ds(0, rr), :].astype(F32)
    resp_out[...] = jnp.concatenate(
        [total[k * RD:(k + 1) * RD] for k in range(heads)], axis=1
    ).astype(BF16)

    for j in range(n_chunks):
        out_copy(j).wait()
        for copy in own(j) + fwd(j):
            copy.wait_send()
    for copy in small:
        copy.wait_send()
    wait_bytes(AG.at[pl.ds(1, n_ctx - 1)], ag_send.at[0])
    wait_bytes(SB.at[pl.ds(1, n_ctx - 1)], r_send.at[0])

    @pl.when(c == 0)
    def _():
        wait_bytes(hidden.at[pl.ds(0, (n_ctx - 1) * ap)], scat_send.at[0])
        wait_bytes(TC.at[pl.ds(0, (n_ctx - 1) * (blk // HD))], scat_send.at[1])


def local(
    ctx_hidden,
    resp_hidden,
    ctx_pos,
    resp_pos,
    input_norm_gain,
    q_weight,
    q_scale,
    k_weight,
    k_scale,
    v_weight,
    v_scale,
):
    n_ctx = lax.axis_size("ctx")
    blk, fs = ctx_hidden.shape
    full, qc = q_weight.shape
    heads = qc // HD
    ap = blk // n_ctx
    rr = heads * RD
    if blk >= 1024:
        sizes = (256, 256, 256, 128, 128)
    else:
        sizes = (blk // 2, blk // 4, blk // 4)
    starts = np.cumsum((0,) + sizes)
    chunks = [(int(a), int(n)) for a, n in zip(starts, sizes)]
    n_chunks = len(chunks)
    top = max(sizes)
    half = np.exp(np.arange(HD // 2, dtype=np.float64) * (-2.0 * math.log(BASE) / HD))
    freq = jnp.asarray(np.concatenate([half, half])[None, :].astype(np.float32))
    vm = pl.BlockSpec(memory_space=pltpu.VMEM)
    hbm = pl.BlockSpec(memory_space=pl.ANY)
    dma = pltpu.SemaphoreType.DMA
    scratch = [
        pltpu.VMEM((full, qc + 2 * HD), BF16),
        pltpu.VMEM((NX, blk, fs), BF16),
        pltpu.VMEM((NX, ap + 16, fs), BF16),
        pltpu.VMEM((top, full), BF16),
        pltpu.VMEM((ap + 16, full), BF16),
        pltpu.VMEM((blk // HD, HD), F32),
        pltpu.VMEM((blk // HD, HD), F32),
        pltpu.VMEM((blk, HD), F32),
        pltpu.VMEM((blk, HD), F32),
        pltpu.VMEM((n_ctx, 2 * ap + rr, HD), BF16),
        pltpu.VMEM((blk, HD), BF16),
        pltpu.VMEM((blk, 2 * HD), BF16),
        pltpu.VMEM((n_ctx * rr, HD), BF16),
        pltpu.VMEM((blk, HD), BF16),
        pltpu.VMEM((blk, 2 * HD), BF16),
        pltpu.VMEM((HD, HD), BF16),
        pltpu.VMEM((HD, 2 * HD), BF16),
        pltpu.VMEM((heads, top, HD), BF16),
        pltpu.VMEM((blk, qc), BF16),
        pltpu.VMEM((n_ctx * rr, HD), F32),
        pltpu.VMEM((n_ctx * rr, 2 * HD), F32),
        pltpu.VMEM((n_ctx, rr + 16, HD), BF16),
        pltpu.VMEM((n_ctx - 1, rr + 16, HD), BF16),
        pltpu.VMEM((n_ctx, HD), F32),
        pltpu.VMEM((HD, HD), F32),
        dma((5,)),
        dma((2,)),
        dma((2,)),
        dma((3,)),
        dma((3,)),
        dma((1,)),
        dma((1,)),
        dma((n_chunks, 4)),
        dma((n_chunks, 4)),
        dma((1,)),
        dma((1,)),
        dma((n_chunks,)),
    ]
    return pl.pallas_call(
        functools.partial(kernel, n_ctx, chunks),
        out_shape=(
            jax.ShapeDtypeStruct((blk, qc), BF16),
            jax.ShapeDtypeStruct((RD, qc), BF16),
        ),
        in_specs=[hbm, vm, vm, vm, vm, hbm, hbm, hbm, vm, vm, vm, vm],
        out_specs=(hbm, vm),
        scratch_shapes=scratch,
        compiler_params=pltpu.CompilerParams(
            collective_id=0, has_side_effects=True, vmem_limit_bytes=60 * 2**20
        ),
    )(
        ctx_hidden,
        resp_hidden,
        ctx_pos.reshape(blk // HD, HD),
        resp_pos.reshape(1, RD),
        input_norm_gain.reshape(1, full),
        q_weight,
        k_weight,
        v_weight,
        q_scale.reshape(1, qc),
        k_scale.reshape(1, HD),
        v_scale.reshape(1, HD),
        freq,
    )


def solution(mesh):
    return jax.shard_map(
        local,
        mesh=mesh,
        in_specs=(
            P("ctx", "head"),
            P("ctx", "head"),
            P("ctx"),
            P("ctx"),
            P(),
            P(None, "head"),
            P("head"),
            P(None, "head"),
            P("head"),
            P(None, "head"),
            P("head"),
        ),
        out_specs=(P("ctx", "head"), P("ctx", "head")),
        check_vma=False,
    )
```

time: 555 us -> 125 us (0.23); the launches traced: 544 us -> 125 us
  other arithmetic: 164 us -> 0 us
  waiting for transfers between devices: 145 us -> 0 us
  Pallas kernels: 0 us -> 121 us
  matrix products: 87.2 us -> 0 us
  blocking collectives: 72.5 us -> 0 us
  local copies, waits for them, and re-layouts: 59 us -> 3.69 us
  between operations: 14.3 us -> 0.65 us
    pallas_call x0 -> x1, Pallas kernels: none -> 121 us  [local(): pl.pallas_call(functools.partial(kernel, n_ctx, chunks), out_shape=(jax.S...]
    all_gather x2 -> x0, waiting for transfers between devices: 105 us -> none  [the longest x1 84.2 us: apply_projection(): whole = lax.all_gather(input_rows, 'head', axis=1, tiled=True)]
    dot_general x11 -> x0, matrix products: 87.2 us -> none  [the longest x2 30.8 us: attend(): jnp.einsum('nkgd,skd->kgns', query_block, key_rows, preferred_element_typ...]
    add x65 -> x0, other arithmetic: 82.6 us -> none  [the longest x31 58.7 us: combine(): left[1] * left_factor[..., None] + right[1] * right_factor[..., None]]
    all_gather x3 -> x0, blocking collectives: 72.5 us -> none  [the longest x2 46.7 us: combined_all(): gathered = jax.tree.map(lambda a: lax.all_gather(a, axis), part)]
    reduce_sum x5 -> x0, other arithmetic: 42 us -> none  [the longest x2 31.9 us: attend(): denom = jnp.sum(weights, axis=-1)]
    psum x1 -> x0, waiting for transfers between devices: 40.1 us -> none  [spread(): return lax.psum(kept, axis)]
    while x42 -> x0, local copies, waits for them, and re-layouts: 36.8 us -> none  [the longest x3 34 us: combined_all(): lax.fori_loop(1, lax.axis_size(axis), lambda source, state: combine(state...]
  transfers between devices with their start and end apart: 3 -> 0, of which waited for: 3 -> 0; matrix products, arithmetic and copies ran while one was open for 23% -> 0% of each run, Pallas kernels for 0% -> 0%
where the time goes in v1:
time: 125 us
  Pallas kernels  121 us (97%)
  local copies, waits for them, and re-layouts  3.69 us (3%)
    pallas_call x1, Pallas kernels, local(): pl.pallas_call(functools.partial(kernel, n_ctx, chunks), out_shape=(jax.S...  121 us
    unnamed x4, local copies, waits for them, and re-layouts  3.69 us

profile of v1, /device:TPU:1, one launch (start us, length us, event | category | flops | bytes accessed | tf_op | source)
XLA Modules:
  0.0 125.2 jit_solution(7486239472915319817)
XLA Ops:
  0.6 120.8 %shard_map.131 = (bf16[1024,1024]{1,0:T(8,128)(2,1)}, bf16[8,1024]{1,0:T(8,128)(2,1)}) custom-call(bf16[1024,1024]{1,0:T(8,128)(2,1)} %hidden.1, bf16[8,1024]{1,0:T(8,128)(2,1)} %resp_hidden.1, s32[8,128]{1,0:T(8,128)} %bitcast.7, s32[1,8]{1,0:T(1,128)} %bitcast.9, f32[1,4096]{1,0:T(1,128)} %bitcast.6, bf16[4096,1024]{1,0:T(8,128)(2,1)} %qw.1, ...), custom_call_target="tpu_custom_call" | custom-call | tf_op jit(solution)/shard_map/pallas_call | solution.py:562
  121.5 0.0 copy-start
  121.5 3.1 %copy.16 = bf16[1024,1024]{1,0:T(8,128)(2,1)} copy(bf16[1024,1024]{1,0:T(8,128)(2,1)} %get-tuple-element.4) | data formatting | bytes 4194304
  124.6 0.0 copy-done
  124.6 0.6 copy.17
Async XLA Ops:
  121.5 3.1 %copy-start = (bf16[8,1024]{1,0:T(8,128)(2,1)S(1)}, bf16[8,1024]{1,0:T(8,128)(2,1)}, u32[]{:S(2)}) copy-start(bf16[8,1024]{1,0:T(8,128)(2,1)} %get-tuple-element.5) | copy-start | bytes 49156
